TPU v7x, 1024 devices: a whole 8x8x8 slice. The times are simulated.
1024 devices in a mesh: dp: 32 (over y, x_lo, core), slab: 32 (over x_hi, z).
Axes of the slice: x: 8 (x_hi: 4, x_lo: 2; x = x_hi * 2 + x_lo), y: 8, z: 8, core: 2. Of those that a mesh axis runs over, the one named last changes fastest.
Arguments:
- features: bfloat16 [32, 320, 64, 256], P('dp', 'slab'), may hold values from -6 to 6
- voxel_mask: int32 [32, 320, 64], P('dp', 'slab'), may hold values 0 or 1
- block_pairs: int32 [32, 32, 27, 10], P('dp', 'slab'), may hold values from 5 to 30, as said below
- cotangent: bfloat16 [32, 320, 64, 128], P('dp', 'slab'), may hold values from -6 to 6
- weight: bfloat16 [27, 256, 128], replicated, may hold values from -0.078125 to 0.078125
Outputs:
- conv_out: bfloat16 [32, 320, 64, 128], P('dp', 'slab')
- input_grad: bfloat16 [32, 320, 64, 256], P('dp', 'slab')
- weight_grad: float32 [27, 256, 128], P(None, 'slab', 'dp')
Inputs may be any that keep to these rules, and one draw needn't show every extreme that they name: `block_pairs`: entries below 10 are at least 5, so they name only the last 5 blocks of the slab below; entries from 20 to below 30 lie under 2*10 + 5, so they name only the first 5 blocks of the slab above; 30 means no block. The first slab never names a slab below it and the last never one above it.
All inputs are finite; a program needn't handle non-finite values. No bound on the sum of `voxel_mask` on one device may be relied on, other than what follows from the above.
Results may differ from a plain program's by a relative error of at most 0.0075.
Values may be sent and summed in bfloat16 or wider, within the bound.
A program may use at most 64 MiB of HBM per device.

v0:
```python
import math

import jax
import jax.numpy as jnp
from jax import lax
from jax.sharding import PartitionSpec as P


def padded_2(shard, sides, width):
    for axis, dim in sides:
        size, length = (lax.axis_size(axis), shard.shape[dim])
        up = [(i, (i + 1) % size) for i in range(size - 1)]
        down = [(j, i) for i, j in up]
        last = lax.slice_in_dim(shard, length - width, length, axis=dim)
        first = lax.slice_in_dim(shard, 0, width, axis=dim)
        before = lax.ppermute(last, axis, up)
        after = lax.ppermute(first, axis, down)
        shard = jnp.concatenate([before, shard, after], axis=dim)
    return shard


def passed_along(value, axis, steps):
    count = lax.axis_size(axis)
    first, last = (max(0, -steps), min(count, count - steps))
    return lax.ppermute(value, axis, [(source, source + steps) for source in range(first, last)])


def per_device(features, voxel_mask, block_pairs, cotangent, weight):
    blocks = features.shape[1]
    slots = features.shape[2]
    in_width = features.shape[3]
    active = voxel_mask[0].astype(jnp.bfloat16)[..., None]
    masked = features[0] * active
    extended = padded_2(masked, (("slab", 0),), blocks)
    padded = jnp.concatenate([extended, jnp.zeros((1, slots, in_width), jnp.bfloat16)], axis=0)
    links = block_pairs[0, 0]
    slot_rows = jnp.where(links == 3 * blocks, blocks + 2 * blocks, links - (blocks - blocks))
    gathered = padded[slot_rows]
    summed = jnp.einsum("kbvc,kco->bvo", gathered, weight, preferred_element_type=jnp.float32)
    conv_out = (summed * active).astype(jnp.bfloat16)
    masked_grad = cotangent[0] * active
    weight_local = jnp.einsum(
        "kbvc,bvo->kco", gathered, masked_grad, preferred_element_type=jnp.float32
    )

    def scatter_offset(adjoint, item):
        rows, weight_k = item
        term = jnp.einsum("bvo,co->bvc", masked_grad, weight_k, preferred_element_type=jnp.float32)
        return (adjoint.at[rows].add(term), None)

    start = jnp.zeros((blocks + 2 * blocks + 1, slots, in_width), jnp.float32)
    adjoint, unused = lax.scan(scatter_offset, start, (slot_rows, weight))
    lower_part = adjoint[:blocks]
    upper_part = adjoint[blocks + blocks : blocks + 2 * blocks]
    from_upper = passed_along(lower_part.astype(jnp.bfloat16), "slab", -1).astype(lower_part.dtype)
    from_lower = passed_along(upper_part.astype(jnp.bfloat16), "slab", 1).astype(upper_part.dtype)
    own_rows = adjoint[blocks : blocks + blocks]
    own_rows = own_rows.at[blocks - blocks :].add(from_upper)
    own_rows = own_rows.at[:blocks].add(from_lower)
    input_grad = (own_rows * active).astype(jnp.bfloat16)
    slab_share = lax.psum_scatter(weight_local, "slab", scatter_dimension=1, tiled=True)
    final_share = lax.psum_scatter(slab_share, "dp", scatter_dimension=2, tiled=True)
    count = lax.axis_size("dp") * lax.axis_size("slab") * blocks * slots
    weight_grad = final_share / jnp.float32(math.sqrt(count))
    return (conv_out[None], input_grad[None], weight_grad)


def solution(mesh):
    placed = (
        P("dp", "slab", None, None),
        P("dp", "slab", None),
        P("dp", "slab", None, None),
        P("dp", "slab", None, None),
        P(),
    )
    return jax.shard_map(
        per_device,
        mesh=mesh,
        in_specs=placed,
        out_specs=(P("dp", "slab", None, None), P("dp", "slab", None, None), P(None, "slab", "dp")),
        check_vma=False,
    )
```

profile of v0, /device:TPU:1, one launch (start us, length us, event | category | flops | bytes accessed | tf_op | source)
XLA Modules:
  0.0 426.1 jit_solution(14475004184322800515)
XLA Ops:
  9.0 5.8 %collective-permute-start = (bf16[10,64,256]{2,1,0:T(8,128)(2,1)S(1)}, bf16[10,64,256]{2,1,0:T(8,128)(2,1)S(1)}, u32[]{:S(2)}, u32[]{:S(2)}) collective-permute-start(bf16[10,64,256]{2,1,0:T(8,128)(2,1)S(1)} %bitcast_multiply_fusion), channel_id=1, source_target_pairs={{0,1},{1,2},{2,3},{3,4},{4,5},{5,6},{6,7},{7,8},{8,9},{9,10},{10,1... | collective-permute-start | bytes 983048 | tf_op jit(solution)/shard_map/ppermute | solution.py:16
  19.0 5.2 %collective-permute-done.1 = bf16[10,64,256]{2,1,0:T(8,128)(2,1)S(1)} collective-permute-done((bf16[10,64,256]{2,1,0:T(8,128)(2,1)S(1)}, bf16[10,64,256]{2,1,0:T(8,128)(2,1)S(1)}, u32[]{:S(2)}, u32[]{:S(2)}) %collective-permute-start.1) | collective-permute-done | bytes 327712 | tf_op jit(solution)/shard_map/ppermute | solution.py:17
  24.3 10.1 %gather_fusion = bf16[270,64,256]{2,1,0:T(8,128)(2,1)} fusion(bf16[31,64,256]{2,1,0:T(8,128)(2,1)S(1)} %maximum_maximum_fusion, s32[1024]{0:T(1024)S(1)} %pad_clamp_fusion), kind=kCustom, calls=%fused_computation | custom fusion | bytes 17695800 | tf_op jit(solution)/shard_map/gather | solution.py:38
  34.4 7.8 %convolution_bitcast_fusion.1 = f32[27,256,128]{2,1,0:T(8,128)} fusion(bf16[27,10,64,256]{3,2,1,0:T(8,128)(2,1)} %bitcast.69, bf16[10,64,128]{2,1,0:T(8,128)(2,1)S(1)} %bitcast_multiply_fusion.1), kind=kOutput, calls=%fused_computation.8 | convolution fusion | flops 1132462080 | bytes 12550144 | tf_op jit(solution)/shard_map/kbvc,bvo->kco/dot_general | solution.py:42
  42.4 66.9 %while.14 = (s32[]{:T(128)}, f32[31,64,256]{2,1,0:T(8,128)S(1)}, s32[27,10]{1,0:T(8,128)S(1)}, bf16[27,256,128]{2,1,0:T(8,128)(2,1)}, bf16[10,64,128]{2,1,0:T(8,128)(2,1)S(1)}, /*index=5*/s32[]{:T(128)}) while((s32[]{:T(128)}, f32[31,64,256]{2,1,0:T(8,128)S(1)}, s32[27,10]{1,0:T(8,128)S(1)}, bf16[27,256,128]{2,1,0:T(8,128)(2,1)}, ...), condition=%wide.region_2.3_spmd, body=%wide.region_0.2_spmd.sunk | while | flops 42106912 | bytes 2851521 | solution.py:52
  51.0 1.3 scatter_fusion
  58.4 1.3 scatter_fusion
  60.9 1.3 scatter_fusion
  65.8 1.3 scatter_fusion
  68.3 1.3 scatter_fusion
  70.8 1.3 scatter_fusion
  73.3 1.3 scatter_fusion
  75.7 1.3 scatter_fusion
  78.2 1.3 scatter_fusion
  80.7 1.4 scatter_fusion
  83.2 1.3 scatter_fusion
  85.7 1.3 scatter_fusion
  88.1 1.3 scatter_fusion
  90.6 1.3 scatter_fusion
  93.1 1.3 scatter_fusion
  95.6 1.3 scatter_fusion
  98.1 1.3 scatter_fusion
  100.6 1.3 scatter_fusion
  103.0 1.3 scatter_fusion
  105.5 1.3 scatter_fusion
  108.0 1.3 scatter_fusion
  109.6 1.4 collective-permute-start.2
  111.0 8.3 %collective-permute-start.3 = (bf16[10,64,256]{2,1,0:T(8,128)(2,1)S(1)}, bf16[10,64,256]{2,1,0:T(8,128)(2,1)S(1)}, u32[]{:S(2)}, u32[]{:S(2)}) collective-permute-start(bf16[10,64,256]{2,1,0:T(8,128)(2,1)S(1)} %get-tuple-element.93), channel_id=1, source_target_pairs={{0,1},{1,2},{2,3},{3,4},{4,5},{5,6},{6,7},{7,8},{8,9},{9,10},{10,1... | collective-permute-start | bytes 983048 | tf_op jit(solution)/shard_map/ppermute | solution.py:25
  119.3 6.7 %fusion.15 = bf16[1,10,64,128]{3,2,1,0:T(8,128)(2,1)} fusion(bf16[27,10,64,256]{3,2,1,0:T(8,128)(2,1)} %bitcast.70, bf16[27,256,128]{2,1,0:T(8,128)(2,1)S(1)} %copy-done, f32[10,64]{1,0:T(8,128)S(1)} %get-tuple-element.90), kind=kOutput, calls=%fused_computation.14 | convolution fusion | flops 1132625920 | bytes 10783232 | tf_op jit(solution)/shard_map/kbvc,kco->bvo/dot_general | solution.py:39
  126.0 167.9 %reduce-scatter.3.cloned.1.call-done = f32[27,8,128]{2,1,0:T(8,128)} async-done(((f32[27,256,128]{2,1,0:T(8,128)}), f32[27,8,128]{2,1,0:T(8,128)}) %reduce-scatter.3.cloned.1.call-update) | async-done | bytes 110608 | tf_op jit(solution)/shard_map/reduce_scatter | solution.py:61
  293.8 1.9 copy.17
  296.7 121.2 %reduce-scatter.5.cloned.1.call-done = f32[27,8,4]{0,1,2:T(8,128)} async-done(((f32[27,8,128]{0,1,2:T(8,128)}), f32[27,8,4]{0,1,2:T(8,128)}) %reduce-scatter.5.cloned.1.call-update) | async-done | bytes 3472 | tf_op jit(solution)/shard_map/reduce_scatter | solution.py:62
  (88 shorter events, 46.5 us)
Async XLA Ops:
  7.2 286.7 %reduce-scatter.3.cloned.1.call-start = ((), (), s32[]{:S(2)}) async-start(), calls=%async_computation.2 | async-start | bytes 3649536 | tf_op jit(solution)/shard_map/reduce_scatter | solution.py:61
  9.0 9.9 %collective-permute-start = (bf16[10,64,256]{2,1,0:T(8,128)(2,1)S(1)}, bf16[10,64,256]{2,1,0:T(8,128)(2,1)S(1)}, u32[]{:S(2)}, u32[]{:S(2)}) collective-permute-start(bf16[10,64,256]{2,1,0:T(8,128)(2,1)S(1)} %bitcast_multiply_fusion), channel_id=1, source_target_pairs={{0,1},{1,2},{2,3},{3,4},{4,5},{5,6},{6,7},{7,8},{8,9},{9,10},{10,1... | collective-permute-start | bytes 983048 | tf_op jit(solution)/shard_map/ppermute | solution.py:16
  14.8 9.4 %collective-permute-start.1 = (bf16[10,64,256]{2,1,0:T(8,128)(2,1)S(1)}, bf16[10,64,256]{2,1,0:T(8,128)(2,1)S(1)}, u32[]{:S(2)}, u32[]{:S(2)}) collective-permute-start(bf16[10,64,256]{2,1,0:T(8,128)(2,1)S(1)} %bitcast_multiply_fusion), channel_id=1, source_target_pairs={{1,0},{2,1},{3,2},{4,3},{5,4},{6,5},{7,6},{8,7},{9,8},{10,9},{11,1... | collective-permute-start | bytes 983048 | tf_op jit(solution)/shard_map/ppermute | solution.py:17
  42.2 375.7 %reduce-scatter.5.cloned.1.call-start = ((), (), s32[]{:S(2)}) async-start(), calls=%async_computation.3 | async-start | bytes 540672 | tf_op jit(solution)/shard_map/reduce_scatter | solution.py:62
  109.4 9.9 %copy-start = (bf16[27,256,128]{2,1,0:T(8,128)(2,1)S(1)}, bf16[27,256,128]{2,1,0:T(8,128)(2,1)}, u32[]{:S(2)}) copy-start(bf16[27,256,128]{2,1,0:T(8,128)(2,1)} %get-tuple-element.158) | copy-start | bytes 5308420
  109.6 186.2 %collective-permute-start.2 = (bf16[10,64,256]{2,1,0:T(8,128)(2,1)S(1)}, bf16[10,64,256]{2,1,0:T(8,128)(2,1)S(1)}, u32[]{:S(2)}, u32[]{:S(2)}) collective-permute-start(bf16[10,64,256]{2,1,0:T(8,128)(2,1)S(1)} %get-tuple-element.92), channel_id=1, source_target_pairs={{1,0},{2,1},{3,2},{4,3},{5,4},{6,5},{7,6},{8,7},{9,8},{10,9},{11,1... | collective-permute-start | bytes 983048 | tf_op jit(solution)/shard_map/ppermute | solution.py:25
  111.0 184.8 %collective-permute-start.3 = (bf16[10,64,256]{2,1,0:T(8,128)(2,1)S(1)}, bf16[10,64,256]{2,1,0:T(8,128)(2,1)S(1)}, u32[]{:S(2)}, u32[]{:S(2)}) collective-permute-start(bf16[10,64,256]{2,1,0:T(8,128)(2,1)S(1)} %get-tuple-element.93), channel_id=1, source_target_pairs={{0,1},{1,2},{2,3},{3,4},{4,5},{5,6},{6,7},{7,8},{8,9},{9,10},{10,1... | collective-permute-start | bytes 983048 | tf_op jit(solution)/shard_map/ppermute | solution.py:25
Sparse Core Ops, SparseCore 0:
  42.3 251.5 reduce-scatter.2
  297.6 120.2 reduce-scatter.4
where the time goes:
time: 428 us; the launch traced here: 426 us
  waiting for transfers between devices  294 us (69%)
  matrix products  43.6 us (10%)
  other arithmetic  42.2 us (10%)
  starting transfers between devices  16.8 us (4%)
  between operations  14.2 us (3%)
  local copies, waits for them, and re-layouts  13.9 us (3%)
    reduce_scatter x1, waiting for transfers between devices, per_device(): lax.psum_scatter(weight_local, 'slab', scatter_dimension=1, tiled=True)  168 us
    reduce_scatter x1, waiting for transfers between devices, per_device(): lax.psum_scatter(slab_share, 'dp', scatter_dimension=2, tiled=True)  121 us
    scatter-add x27, other arithmetic, scatter_offset(): return (adjoint.at[rows].add(term), None)  36.4 us
    dot_general x27, matrix products, scatter_offset(): jnp.einsum('bvo,co->bvc', masked_grad, weight_k, preferred_element_type=j...  29.2 us
    gather x1, local copies, waits for them, and re-layouts, per_device(): gathered = padded[slot_rows]  10.1 us
    ppermute x2, starting transfers between devices, passed_along(): lax.ppermute(value, axis, [(source, source + steps) for source in range(f...  9.71 us
  transfers between devices with their start and end apart: 6, of which 3 were waited for; matrix products, arithmetic and copies ran while one was open for 18% of the time, Pallas kernels for 0%

commit v1 on v0

v1 whole, which is shorter than its diff:
```python
import math

import jax
import jax.numpy as jnp
from jax import lax
from jax.experimental import pallas as pl
from jax.experimental.pallas import tpu as pltpu
from jax.sharding import PartitionSpec as P

MESH = pl.DeviceIdType.MESH
F32 = jnp.float32
BF16 = jnp.bfloat16

OFFSETS = 27
BLOCKS = 10
RIM = 5
VOX = 64
CIN = 256
COUT = 128
ROWS = BLOCKS * VOX
SIDE = 8
SLOTS = 14
HALF = 7
ZERO = BLOCKS + 2 * RIM


def dot(a, b):
    return jnp.dot(a, b, preferred_element_type=F32)


def dot_nt(a, b):
    return lax.dot_general(a, b, (((1,), (1,)), ((), ())), preferred_element_type=F32)


def one_hot(rows, source):
    r = lax.broadcasted_iota(jnp.int32, (rows, rows), 0)
    c = lax.broadcasted_iota(jnp.int32, (rows, rows), 1)
    return jnp.where(c == source(r), 1.0, 0.0).astype(BF16)


def adjoint_kernel(idx, grad, weight, own, low, up, acc):
    acc[...] = jnp.zeros_like(acc)

    def step(i, carry):
        for u in range(3):
            k = i * 3 + u
            term = dot_nt(grad[...], weight[k])
            for b in range(BLOCKS):
                row = idx[k * BLOCKS + b]
                acc[row] = acc[row] + term[b * VOX : (b + 1) * VOX]
        return carry

    lax.fori_loop(0, OFFSETS // 3, step, 0)
    low[...] = acc[0:RIM].astype(BF16)
    own[...] = acc[RIM : RIM + BLOCKS]
    up[...] = acc[RIM + BLOCKS : ZERO].astype(BF16)


def main_kernel(
    idx, masked, grad, active, weight, own_adj, low_adj, up_adj,
    conv_out, input_grad, pieces,
    ext, adj_low, adj_up, grad_t, conv_acc, kept,
    core_send, core_recv, y_send, y_recv, z_send, z_recv,
    yz_send, yz_recv, zy_send, zy_recv, x_send, x_recv,
    halo_ssem, halo_rsem, core_ssem, core_rsem,
    y_ssem, y_rsem, z_ssem, z_rsem, yz_ssem, yz_rsem, zy_ssem, zy_rsem, x_ssem, x_rsem,
):
    dp = lax.axis_index("dp")
    slab = lax.axis_index("slab")
    y, x_lo, core = dp // 4, (dp // 2) % 2, dp % 2
    x_hi, z = slab // SIDE, slab % SIDE
    x = x_hi * 2 + x_lo

    def device(y, x, z, core):
        return {"dp": y * 4 + (x % 2) * 2 + core, "slab": (x // 2) * SIDE + z}

    mate = device(y, x, z, 1 - core)
    above = {"dp": dp, "slab": (slab + 1) % 32}
    below = {"dp": dp, "slab": (slab + 31) % 32}
    y_at = [(y + d) % SIDE for d in range(SIDE)]
    z_at = [(z + d) % SIDE for d in range(SIDE)]
    x_at = [(x + d) % SIDE for d in range(SIDE)]
    y_peer = [device(y_at[d], x, z, core) for d in range(SIDE)]
    z_peer = [device(y, x, z_at[d], core) for d in range(SIDE)]
    x_peer = [(x_at[d], device(y, x_at[d], z, (core + c) % 2)) for d in range(SIDE) for c in range(2)]

    barrier = pltpu.get_barrier_semaphore()
    others = [above, below] + y_peer[1:] + z_peer[1:] + [p for _, p in x_peer[1:]]
    for other in others:
        pl.semaphore_signal(barrier, inc=1, device_id=other, device_id_type=MESH)
    pl.semaphore_wait(barrier, len(others))

    def remote(src, dst, ssem, rsem, to):
        return pltpu.make_async_remote_copy(
            src_ref=src, dst_ref=dst, send_sem=ssem, recv_sem=rsem, device_id=to, device_id_type=MESH
        )

    halos = [
        remote(masked.at[pl.ds(RIM, RIM)], ext.at[pl.ds(0, RIM)], halo_ssem.at[0], halo_rsem.at[0], above),
        remote(masked.at[pl.ds(0, RIM)], ext.at[pl.ds(RIM + BLOCKS, RIM)], halo_ssem.at[1], halo_rsem.at[1], below),
        remote(low_adj, adj_up, halo_ssem.at[2], halo_rsem.at[2], below),
        remote(up_adj, adj_low, halo_ssem.at[3], halo_rsem.at[3], above),
    ]
    for copy in halos:
        copy.start()
    ext[RIM : RIM + BLOCKS] = masked[...]
    ext[ZERO] = jnp.zeros((VOX, CIN), BF16)
    grad_t[...] = dot_nt(one_hot(COUT, lambda r: r), grad[...]).astype(BF16)
    halos[0].wait_recv()
    halos[1].wait_recv()

    def picked(k, first, last):
        return jnp.concatenate([ext[idx[k * BLOCKS + b]] for b in range(first, last)], axis=0)

    def kernel_grad(k):
        total = None
        for first, last in ((0, 4), (4, 8), (8, 10)):
            part = dot(grad_t[:, first * VOX : last * VOX], picked(k, first, last))
            total = part if total is None else total + part
        return total

    def to_mate(j):
        return remote(core_send.at[j], core_recv.at[j], core_ssem.at[j], core_rsem.at[j], mate)

    def both_terms(j, carry):
        core_send[j] = kernel_grad((1 - core) * SLOTS + j).astype(BF16)
        to_mate(j).start()
        kept[j] = kernel_grad(core * SLOTS + j)
        return carry

    def chip_sum(j):
        to_mate(j).wait_recv()
        return (kept[j] + core_recv[j].astype(F32)).astype(BF16)

    lax.fori_loop(0, HALF, both_terms, 0)

    def y_slot(j, carry):
        y_send[j] = chip_sum(j)
        return carry

    lax.fori_loop(0, HALF, y_slot, 0)
    y_copy = [
        remote(
            y_send.at[:, pl.ds(pl.multiple_of(y_at[d] * 16, 16), 16), :],
            y_recv.at[d - 1], y_ssem.at[d - 1], y_rsem.at[d - 1], y_peer[d],
        )
        for d in range(1, SIDE)
    ]
    for copy in y_copy:
        copy.start()

    lax.fori_loop(HALF, SLOTS, both_terms, 0)
    by_z = one_hot(CIN, lambda r: ((r // 8) % 4) * 64 + (r // 32) * 8 + r % 8)

    def z_slot(j, carry):
        z_send[j] = dot_nt(by_z, chip_sum(j + HALF)).astype(BF16)
        return carry

    lax.fori_loop(0, HALF, z_slot, 0)
    z_copy = [
        remote(
            z_send.at[:, pl.ds(pl.multiple_of(z_at[d] * 32, 32), 32), :],
            z_recv.at[d - 1], z_ssem.at[d - 1], z_rsem.at[d - 1], z_peer[d],
        )
        for d in range(1, SIDE)
    ]
    for copy in z_copy:
        copy.start()

    conv_acc[...] = jnp.zeros_like(conv_acc)

    def conv_step(i, carry):
        for u in range(3):
            k = i * 3 + u
            conv_acc[...] = conv_acc[...] + dot(picked(k, 0, BLOCKS), weight[k])
        return carry

    lax.fori_loop(0, OFFSETS // 3, conv_step, 0)
    live = active[...].astype(F32)
    conv_out[...] = (conv_acc[...] * live).astype(BF16)

    halos[2].wait_recv()
    halos[3].wait_recv()
    for b in range(BLOCKS):
        if b < RIM:
            extra = adj_low[b]
        else:
            extra = adj_up[b - RIM]
        lb = live[b * VOX : (b + 1) * VOX]
        total = own_adj[b] + extra.astype(F32)
        input_grad[b] = (total * jnp.concatenate([lb, lb], axis=1)).astype(BF16)

    for copy in y_copy:
        copy.wait_recv()
    total = y_send[:, pl.ds(pl.multiple_of(y * 16, 16), 16), :].astype(F32)
    for d in range(1, SIDE):
        total = total + y_recv[d - 1].astype(F32)
    flat = jnp.concatenate([total.astype(BF16).reshape(HALF * 16, CIN), jnp.zeros((16, CIN), BF16)], axis=0)
    yz_send[...] = dot_nt(by_z, flat).astype(BF16)
    yz_copy = [
        remote(
            yz_send.at[pl.ds(pl.multiple_of(z_at[d] * 32, 32), 32), :],
            yz_recv.at[d - 1], yz_ssem.at[d - 1], yz_rsem.at[d - 1], z_peer[d],
        )
        for d in range(1, SIDE)
    ]
    for copy in yz_copy:
        copy.start()

    for copy in z_copy:
        copy.wait_recv()
    total = z_send[:, pl.ds(pl.multiple_of(z * 32, 32), 32), :].astype(F32)
    for d in range(1, SIDE):
        total = total + z_recv[d - 1].astype(F32)
    flat = jnp.concatenate([total.astype(BF16).reshape(HALF * 32, COUT), jnp.zeros((32, COUT), BF16)], axis=0)
    zy_send[...] = dot_nt(one_hot(COUT, lambda r: r), flat).astype(BF16)
    zy_copy = [
        remote(
            zy_send.at[pl.ds(pl.multiple_of(y_at[d] * 16, 16), 16), :],
            zy_recv.at[d - 1], zy_ssem.at[d - 1], zy_rsem.at[d - 1], y_peer[d],
        )
        for d in range(1, SIDE)
    ]
    for copy in zy_copy:
        copy.start()

    for copy in yz_copy:
        copy.wait_recv()
    first = yz_send[pl.ds(pl.multiple_of(z * 32, 32), 32), :].astype(F32)
    for d in range(1, SIDE):
        first = first + yz_recv[d - 1].astype(F32)
    for copy in zy_copy:
        copy.wait_recv()
    second = zy_send[pl.ds(pl.multiple_of(y * 16, 16), 16), :].astype(F32)
    for d in range(1, SIDE):
        second = second + zy_recv[d - 1].astype(F32)
    for i in range(SIDE):
        hi, lo = i // 2, i % 2
        x_send[i, :, 0:128] = first[hi * 8 : hi * 8 + 8]
        x_send[i, :, 128:384] = second[lo * 8 : lo * 8 + 8]
    x_copy = [
        remote(x_send.at[at], x_recv.at[n], x_ssem.at[n], x_rsem.at[n], to)
        for n, (at, to) in enumerate(x_peer[1:])
    ]
    for copy in x_copy:
        copy.start()
    for copy in x_copy:
        copy.wait_recv()
    mine = x_send[x]
    for d in range(1, SIDE):
        mine = mine + x_recv[2 * d - 1]
    theirs = x_recv[0]
    for d in range(1, SIDE):
        theirs = theirs + x_recv[2 * d]
    pieces[core] = mine
    pieces[1 - core] = theirs

    for copy in halos + y_copy + z_copy + yz_copy + zy_copy + x_copy:
        copy.wait_send()

    def sent(j, carry):
        to_mate(j).wait_send()
        return carry

    lax.fori_loop(0, SLOTS, sent, 0)


def per_device(features, voxel_mask, block_pairs, cotangent, weight):
    active = voxel_mask.reshape(BLOCKS, VOX, 1).astype(BF16)
    masked = features[0] * active
    grad = (cotangent[0] * active).reshape(ROWS, COUT)
    live = jnp.broadcast_to(active, (BLOCKS, VOX, COUT)).reshape(ROWS, COUT)
    links = block_pairs.reshape(OFFSETS * BLOCKS)
    idx = jnp.where(links == 3 * BLOCKS, ZERO, links - RIM)
    idx = jnp.concatenate([idx, jnp.full((BLOCKS,), ZERO, jnp.int32)])

    smem = pl.BlockSpec(memory_space=pltpu.SMEM)
    vmem = pl.BlockSpec(memory_space=pltpu.VMEM)
    dma = pltpu.SemaphoreType.DMA
    rim = jax.ShapeDtypeStruct((RIM, VOX, CIN), BF16)
    own, low, up = pl.pallas_call(
        adjoint_kernel,
        out_shape=(jax.ShapeDtypeStruct((BLOCKS, VOX, CIN), F32), rim, rim),
        in_specs=[smem, vmem, vmem],
        out_specs=(vmem, vmem, vmem),
        scratch_shapes=[pltpu.VMEM((ZERO + 1, VOX, CIN), F32)],
        compiler_params=pltpu.CompilerParams(vmem_limit_bytes=32 * 1024 * 1024),
        name="adjoint",
    )(idx, grad, weight)

    conv_out, input_grad, pieces = pl.pallas_call(
        main_kernel,
        out_shape=(
            jax.ShapeDtypeStruct((ROWS, COUT), BF16),
            jax.ShapeDtypeStruct((BLOCKS, VOX, CIN), BF16),
            jax.ShapeDtypeStruct((2, 8, 384), F32),
        ),
        in_specs=[smem] + [vmem] * 7,
        out_specs=(vmem, vmem, vmem),
        scratch_shapes=[
            pltpu.VMEM((ZERO + 1, VOX, CIN), BF16),
            pltpu.VMEM((RIM, VOX, CIN), BF16),
            pltpu.VMEM((RIM, VOX, CIN), BF16),
            pltpu.VMEM((COUT, ROWS), BF16),
            pltpu.VMEM((ROWS, COUT), F32),
            pltpu.VMEM((SLOTS, COUT, CIN), F32),
            pltpu.VMEM((SLOTS, COUT, CIN), BF16),
            pltpu.VMEM((SLOTS, COUT, CIN), BF16),
            pltpu.VMEM((HALF, COUT, CIN), BF16),
            pltpu.VMEM((SIDE - 1, HALF, 16, CIN), BF16),
            pltpu.VMEM((HALF, CIN, COUT), BF16),
            pltpu.VMEM((SIDE - 1, HALF, 32, COUT), BF16),
            pltpu.VMEM((CIN, 128), BF16),
            pltpu.VMEM((SIDE - 1, 32, 128), BF16),
            pltpu.VMEM((COUT, 256), BF16),
            pltpu.VMEM((SIDE - 1, 16, 256), BF16),
            pltpu.VMEM((SIDE, 8, 384), F32),
            pltpu.VMEM((15, 8, 384), F32),
            dma((4,)), dma((4,)), dma((SLOTS,)), dma((SLOTS,)),
            dma((7,)), dma((7,)), dma((7,)), dma((7,)),
            dma((7,)), dma((7,)), dma((7,)), dma((7,)),
            dma((15,)), dma((15,)),
        ],
        compiler_params=pltpu.CompilerParams(
            collective_id=0, has_side_effects=True, vmem_limit_bytes=40 * 1024 * 1024
        ),
        name="conv_and_sums",
    )(idx, masked, grad, live, weight, own, low, up)

    dp, slab = lax.axis_index("dp"), lax.axis_index("slab")
    x_lo, core, x_hi = (dp // 2) % 2, dp % 2, slab // SIDE
    by_y = pieces[:, :, :128].reshape(2, 8, 8, 2, 2, 4)
    by_y = lax.dynamic_index_in_dim(by_y, x_lo, 3, keepdims=False)
    by_y = lax.dynamic_index_in_dim(by_y, core, 3, keepdims=False)
    by_z = pieces[:, :, 128:].reshape(2, 2, 4, 8, 4, 8)
    by_z = lax.dynamic_index_in_dim(by_z, core, 1, keepdims=False)
    by_z = lax.dynamic_index_in_dim(by_z, x_hi, 3, keepdims=False)
    share = jnp.concatenate(
        [by_y.transpose(0, 2, 1, 3)[:, :HALF], by_z.transpose(0, 2, 3, 1)[:, :HALF]], axis=1
    ).reshape(2 * SLOTS, 8, 4)[:OFFSETS]
    count = lax.axis_size("dp") * lax.axis_size("slab") * ROWS
    weight_grad = share / jnp.float32(math.sqrt(count))
    return (conv_out.reshape(1, BLOCKS, VOX, COUT), input_grad[None], weight_grad)


def solution(mesh):
    placed = (
        P("dp", "slab", None, None),
        P("dp", "slab", None),
        P("dp", "slab", None, None),
        P("dp", "slab", None, None),
        P(),
    )
    return jax.shard_map(
        per_device,
        mesh=mesh,
        in_specs=placed,
        out_specs=(P("dp", "slab", None, None), P("dp", "slab", None, None), P(None, "slab", "dp")),
        check_vma=False,
    )
```

time: 428 us -> 84.5 us (0.20)
  waiting for transfers between devices: 294 us -> 0 us
  Pallas kernels: 0 us -> 74.2 us
  matrix products: 43.6 us -> 0 us
  other arithmetic: 42.2 us -> 4.38 us
  starting transfers between devices: 16.8 us -> 0 us
  between operations: 14.2 us -> 0.82 us
  local copies, waits for them, and re-layouts: 13.9 us -> 4.72 us
    reduce_scatter x2 -> x0, waiting for transfers between devices: 289 us -> none  [the longest x1 168 us: per_device(): lax.psum_scatter(weight_local, 'slab', scatter_dimension=1, tiled=True)]
    pallas_call x0 -> x2, Pallas kernels: none -> 74.2 us  [the longest x1 69 us: per_device(): pl.pallas_call(main_kernel, out_shape=(jax.ShapeDtypeStruct((ROWS, COUT),...]
    dot_general x29 -> x0, matrix products: 43.6 us -> none  [the longest x27 29.2 us: scatter_offset(): jnp.einsum('bvo,co->bvc', masked_grad, weight_k, preferred_element_type=j...]
    scatter-add x27 -> x0, other arithmetic: 36.4 us -> none  [scatter_offset(): return (adjoint.at[rows].add(term), None)]
    ppermute x4 -> x0, starting transfers between devices: 16.8 us -> none  [the longest x2 9.71 us: passed_along(): lax.ppermute(value, axis, [(source, source + steps) for source in range(f...]
    gather x1 -> x0, local copies, waits for them, and re-layouts: 10.1 us -> none  [per_device(): gathered = padded[slot_rows]]
    ppermute x4 -> x0, waiting for transfers between devices: 5.2 us -> none  [the longest x1 5.19 us: padded_2(): after = lax.ppermute(first, axis, down)]
  transfers between devices with their start and end apart: 6 -> 0, of which waited for: 3 -> 0; matrix products, arithmetic and copies ran while one was open for 18% -> 0% of each run, Pallas kernels for 0% -> 0%
where the time goes in v1:
time: 84.5 us; the launch traced here: 84.1 us
  Pallas kernels  74.2 us (88%)
  local copies, waits for them, and re-layouts  4.72 us (6%)
  other arithmetic  4.38 us (5%)
    pallas_call x1, Pallas kernels, per_device(): pl.pallas_call(main_kernel, out_shape=(jax.ShapeDtypeStruct((ROWS, COUT),...  69 us
    pallas_call x1, Pallas kernels, per_device(): pl.pallas_call(adjoint_kernel, out_shape=(jax.ShapeDtypeStruct((BLOCKS, V...  5.2 us
    unnamed x8, local copies, waits for them, and re-layouts  3.48 us

profile of v1, /device:TPU:1, one launch (start us, length us, event | category | flops | bytes accessed | tf_op | source)
XLA Modules:
  0.0 84.1 jit_solution(7150220284772860356)
XLA Ops:
  0.6 0.7 compare_select_fusion
  1.3 0.1 copy.13
  1.4 0.1 select_n.46
  1.5 0.7 convert_element_type.15
  2.2 1.1 %bitcast_multiply_fusion.masked = bf16[10,64,256]{2,1,0:T(8,128)(2,1)S(1)} fusion(bf16[1,10,64,256]{3,2,1,0:T(8,128)(2,1)} %param.5, bf16[10,64]{1,0:T(8,128)(2,1)S(1)} %bitcast.27), kind=kLoop, calls=%fused_computation | loop fusion | flops 163840 | bytes 656640 | tf_op jit(solution)/shard_map/mul | solution.py:270
  3.4 0.7 convert_reduce_fusion
  4.1 0.1 convert_element_type.17
  4.2 1.1 %bitcast_multiply_fusion.1.grad = bf16[640,128]{1,0:T(8,128)(2,1)S(1)} fusion(bf16[1,10,64,128]{3,2,1,0:T(8,128)(2,1)} %param.8, bf16[640]{0:T(1024)(128)(2,1)S(1)} %convert_element_type.17), kind=kLoop, calls=%fused_computation.1 | loop fusion | flops 81920 | bytes 328960 | tf_op jit(solution)/shard_map/mul | solution.py:271
  5.2 0.1 mul.19.active
  5.4 0.0 copy-start
  5.4 1.5 %copy-done = bf16[27,256,128]{2,1,0:T(8,128)(2,1)S(1)} copy-done((bf16[27,256,128]{2,1,0:T(8,128)(2,1)S(1)}, bf16[27,256,128]{2,1,0:T(8,128)(2,1)}, u32[]{:S(2)}) %copy-start) | copy-done | bytes 1769496
  6.9 0.0 copy-start.1
  6.9 5.2 %adjoint.1 = (f32[10,64,256]{2,1,0:T(8,128)S(1)}, bf16[5,64,256]{2,1,0:T(8,128)(2,1)S(1)}, bf16[5,64,256]{2,1,0:T(8,128)(2,1)S(1)}) custom-call(s32[280]{0:T(512)S(1)} %concatenate.6.idx, bf16[640,128]{1,0:T(8,128)(2,1)S(1)} %bitcast_multiply_fusion.1.grad, bf16[27,256,128]{2,1,0:T(8,128)(2,1)S(1)} %copy-done), custom_call_target="tpu_custom_call" | custom-call | tf_op jit(solution)/shard_map/adjoint/pallas_call | solution.py:281
  12.1 0.0 copy-done.1
  12.1 69.0 %conv_and_sums.1 = (bf16[640,128]{1,0:T(8,128)(2,1)S(1)}, bf16[10,64,256]{2,1,0:T(8,128)(2,1)S(1)}, f32[2,8,384]{2,1,0:T(8,128)S(1)}) custom-call(s32[280]{0:T(512)S(1)} %concatenate.6.idx, bf16[10,64,256]{2,1,0:T(8,128)(2,1)S(1)} %bitcast_multiply_fusion.masked, bf16[640,128]{1,0:T(8,128)(2,1)S(1)} %bitcast_multiply_fusion.1.grad, ...), custom_call_target="tpu_custom_call" | custom-call | tf_op jit(solution)/shard_map/conv_and_sums/pallas_call | solution.py:291
  81.1 0.3 reshape.49
  81.6 0.1 copy.17
  81.6 0.1 copy.14
  81.8 0.1 copy.15
  81.9 0.1 pad_maximum_fusion
  82.0 0.1 reshape.50
  82.1 0.6 copy.19
  82.7 0.7 copy.26
  83.4 0.7 copy.27
  (8 shorter events, 0.1 us)
Async XLA Ops:
  5.4 1.5 %copy-start = (bf16[27,256,128]{2,1,0:T(8,128)(2,1)S(1)}, bf16[27,256,128]{2,1,0:T(8,128)(2,1)}, u32[]{:S(2)}) copy-start(bf16[27,256,128]{2,1,0:T(8,128)(2,1)} %weight.3) | copy-start | bytes 5308420
  6.9 5.2 %copy-start.1 = (bf16[27,256,128]{2,1,0:T(8,128)(2,1)S(1)}, bf16[27,256,128]{2,1,0:T(8,128)(2,1)}, u32[]{:S(2)}) copy-start(bf16[27,256,128]{2,1,0:T(8,128)(2,1)} %weight.3) | copy-start | bytes 5308420

commit v2 on v1

v2 whole, which is shorter than its diff:
```python
import math

import jax
import jax.numpy as jnp
from jax import lax
from jax.experimental import pallas as pl
from jax.experimental.pallas import tpu as pltpu
from jax.sharding import PartitionSpec as P

MESH = pl.DeviceIdType.MESH
F32 = jnp.float32
BF16 = jnp.bfloat16

OFFSETS = 27
BLOCKS = 10
RIM = 5
VOX = 64
CIN = 256
COUT = 128
ROWS = BLOCKS * VOX
PAIRS = OFFSETS * BLOCKS
SIDE = 8
SLOTS = 14
HALF = 7
ZERO = BLOCKS + 2 * RIM
CHUNKS = ((0, 3), (3, 5), (5, 7))


def dot(a, b):
    return jnp.dot(a, b, preferred_element_type=F32)


def dot_nt(a, b):
    return lax.dot_general(a, b, (((1,), (1,)), ((), ())), preferred_element_type=F32)


def one_hot(rows, cols, match):
    r = lax.broadcasted_iota(jnp.int32, (rows, cols), 0)
    c = lax.broadcasted_iota(jnp.int32, (rows, cols), 1)
    return jnp.where(match(r, c), 1.0, 0.0).astype(BF16)


def main_kernel(
    idx, order, ends, features_hbm, mask_hbm, cotangent_hbm, weight_hbm,
    conv_hbm, input_grad_hbm, pieces,
    conv_out, input_grad, features, mask, cotangent, weight, live, ext, grad, grad_t, term, run, rim_low, rim_up, adj_low, adj_up, conv_acc,
    by_z, pick_y, pick_z, core_send, core_recv, y_send, y_recv, z_send, z_recv,
    yz_send, yz_recv, zy_send, zy_recv, x_send, x_recv,
    load_sem, out_sem, halo_ssem, halo_rsem, core_ssem, core_rsem,
    y_ssem, y_rsem, z_ssem, z_rsem, yz_ssem, yz_rsem, zy_ssem, zy_rsem, x_ssem, x_rsem,
):
    dp = lax.axis_index("dp")
    slab = lax.axis_index("slab")
    y, x_lo, core = dp // 4, (dp // 2) % 2, dp % 2
    x_hi, z = slab // SIDE, slab % SIDE
    x = x_hi * 2 + x_lo

    def device(y, x, z, core):
        return {"dp": y * 4 + (x % 2) * 2 + core, "slab": (x // 2) * SIDE + z}

    mate = device(y, x, z, 1 - core)
    above = {"dp": dp, "slab": (slab + 1) % 32}
    below = {"dp": dp, "slab": (slab + 31) % 32}
    y_at = [(y + d) % SIDE for d in range(SIDE)]
    z_at = [(z + d) % SIDE for d in range(SIDE)]
    x_at = [(x + d) % SIDE for d in range(SIDE)]
    y_peer = [device(y_at[d], x, z, core) for d in range(SIDE)]
    z_peer = [device(y, x, z_at[d], core) for d in range(SIDE)]
    x_peer = [(x_at[d], device(y, x_at[d], z, (core + c) % 2)) for d in range(SIDE) for c in range(2)]

    pairs = ((mask_hbm, mask), (features_hbm, features), (cotangent_hbm, cotangent), (weight_hbm, weight))
    loads = [pltpu.make_async_copy(src, dst, load_sem.at[n]) for n, (src, dst) in enumerate(pairs)]
    for load in loads:
        load.start()
    barrier = pltpu.get_barrier_semaphore()
    others = [above, below] + y_peer[1:] + z_peer[1:] + [p for _, p in x_peer[1:]]
    for other in others:
        pl.semaphore_signal(barrier, inc=1, device_id=other, device_id_type=MESH)

    loads[0].wait()
    loads[1].wait()
    eye = one_hot(VOX, VOX, lambda r, c: r == c)
    rows = jnp.concatenate([mask[b] for b in range(BLOCKS)], axis=0)
    columns = dot_nt(eye, rows.astype(F32).astype(BF16)).astype(BF16)
    for b in range(BLOCKS):
        spread = dot(columns, one_hot(BLOCKS, COUT, lambda r, c: r == b)).astype(BF16)
        live[b] = spread
        ext[RIM + b] = features[0, b] * jnp.concatenate([spread, spread], axis=1)
    ext[ZERO] = jnp.zeros((VOX, CIN), BF16)
    pl.semaphore_wait(barrier, len(others))

    def remote(src, dst, ssem, rsem, to):
        return pltpu.make_async_remote_copy(
            src_ref=src, dst_ref=dst, send_sem=ssem, recv_sem=rsem, device_id=to, device_id_type=MESH
        )

    halos = [
        remote(ext.at[pl.ds(BLOCKS, RIM)], ext.at[pl.ds(0, RIM)], halo_ssem.at[0], halo_rsem.at[0], above),
        remote(ext.at[pl.ds(RIM, RIM)], ext.at[pl.ds(RIM + BLOCKS, RIM)], halo_ssem.at[1], halo_rsem.at[1], below),
        remote(rim_low, adj_up, halo_ssem.at[2], halo_rsem.at[2], below),
        remote(rim_up, adj_low, halo_ssem.at[3], halo_rsem.at[3], above),
    ]
    halos[0].start()
    halos[1].start()

    loads[2].wait()
    for b in range(BLOCKS):
        grad[b * VOX : (b + 1) * VOX] = cotangent[0, b] * live[b]
    grad_t[...] = dot_nt(one_hot(COUT, COUT, lambda r, c: r == c), grad[...]).astype(BF16)
    by_z[...] = one_hot(CIN, CIN, lambda r, c: c == ((r // 8) % 4) * 64 + (r // 32) * 8 + r % 8)
    loads[3].wait()

    def term_step(i, carry):
        for u in range(3):
            k = i * 3 + u
            product = dot_nt(grad[...], weight[k]).astype(BF16)
            term[pl.ds(k * BLOCKS, BLOCKS)] = product.reshape(BLOCKS, VOX, CIN)
        return carry

    lax.fori_loop(0, OFFSETS // 3, term_step, 0)

    def run_step(i, total):
        for u in range(5):
            s = i * 5 + u
            here = order[s]
            last = order[jnp.maximum(s - 1, 0)]
            keep = jnp.where(idx[here] == idx[last], 1.0, 0.0)
            total = total * keep + term[here].astype(F32)
            run[s] = total
        return total

    lax.fori_loop(0, PAIRS // 5, run_step, jnp.zeros((VOX, CIN), F32))

    def target_sum(i):
        found = jnp.where(ends[i + 1] > ends[i], 1.0, 0.0)
        return run[jnp.maximum(ends[i + 1] - 1, 0)] * found

    for i in range(RIM):
        rim_low[i] = target_sum(i).astype(BF16)
        rim_up[i] = target_sum(RIM + BLOCKS + i).astype(BF16)
    halos[0].wait_recv()
    halos[1].wait_recv()

    def picked(k, first, last):
        return jnp.concatenate([ext[idx[k * BLOCKS + b]] for b in range(first, last)], axis=0)

    def kernel_grad(k):
        total = None
        for first, last in ((0, 4), (4, 8), (8, 10)):
            part = dot(grad_t[:, first * VOX : last * VOX], picked(k, first, last))
            total = part if total is None else total + part
        return total

    def to_mate(j):
        return remote(core_send.at[j], core_recv.at[j], core_ssem.at[j], core_rsem.at[j], mate)

    def give(j, carry):
        core_send[j] = kernel_grad((1 - core) * SLOTS + j).astype(BF16)
        to_mate(j).start()
        return carry

    for first, last in CHUNKS:
        lax.fori_loop(first, last, give, 0)
        lax.fori_loop(HALF + first, HALF + last, give, 0)

    def chip_sum(j):
        own = kernel_grad(core * SLOTS + j)
        to_mate(j).wait_recv()
        return (own + core_recv[j].astype(F32)).astype(BF16)

    def y_slot(j, carry):
        y_send[j] = chip_sum(j)
        return carry

    def z_slot(j, carry):
        z_send[j] = dot_nt(by_z[...], chip_sum(j + HALF)).astype(BF16)
        return carry

    y_copy, z_copy = [], []
    for n, (first, last) in enumerate(CHUNKS):
        part = pl.ds(first, last - first)
        lax.fori_loop(first, last, y_slot, 0)
        for d in range(1, SIDE):
            rows = pl.ds(pl.multiple_of(y_at[d] * 16, 16), 16)
            copy = remote(
                y_send.at[part, rows, :], y_recv.at[d - 1, part],
                y_ssem.at[n, d - 1], y_rsem.at[n, d - 1], y_peer[d],
            )
            copy.start()
            y_copy.append(copy)
        lax.fori_loop(first, last, z_slot, 0)
        for d in range(1, SIDE):
            rows = pl.ds(pl.multiple_of(z_at[d] * 32, 32), 32)
            copy = remote(
                z_send.at[part, rows, :], z_recv.at[d - 1, part],
                z_ssem.at[n, d - 1], z_rsem.at[n, d - 1], z_peer[d],
            )
            copy.start()
            z_copy.append(copy)
    halos[2].start()
    halos[3].start()

    conv_acc[...] = jnp.zeros_like(conv_acc)

    def conv_step(i, carry):
        for u in range(3):
            k = i * 3 + u
            conv_acc[...] = conv_acc[...] + dot(picked(k, 0, BLOCKS), weight[k])
        return carry

    lax.fori_loop(0, OFFSETS // 3, conv_step, 0)
    for b in range(BLOCKS):
        conv_out[b] = (conv_acc[b * VOX : (b + 1) * VOX] * live[b].astype(F32)).astype(BF16)
    conv_done = pltpu.make_async_copy(conv_out, conv_hbm, out_sem.at[0])
    conv_done.start()
    pick_y[...] = one_hot(
        128, 256, lambda r, c: (c % 128 < 64) & (r == ((c % 64) // 8) * 16 + (c // 128) * 8 + c % 8)
    )
    pick_z[...] = one_hot(
        256, 512, lambda r, c: (c % 128 >= 64) & (r == ((c % 64) // 8) * 32 + (c // 128) * 8 + c % 8)
    )

    for copy in y_copy:
        copy.wait_recv()
    total = y_send[:, pl.ds(pl.multiple_of(y * 16, 16), 16), :].astype(F32)
    for d in range(1, SIDE):
        total = total + y_recv[d - 1].astype(F32)
    flat = jnp.concatenate([total.astype(BF16).reshape(HALF * 16, CIN), jnp.zeros((16, CIN), BF16)], axis=0)
    yz_send[...] = dot_nt(by_z[...], flat).astype(BF16)
    yz_copy = [
        remote(
            yz_send.at[pl.ds(pl.multiple_of(z_at[d] * 32, 32), 32), :],
            yz_recv.at[d - 1], yz_ssem.at[d - 1], yz_rsem.at[d - 1], z_peer[d],
        )
        for d in range(1, SIDE)
    ]
    for copy in yz_copy:
        copy.start()

    for copy in z_copy:
        copy.wait_recv()
    total = z_send[:, pl.ds(pl.multiple_of(z * 32, 32), 32), :].astype(F32)
    for d in range(1, SIDE):
        total = total + z_recv[d - 1].astype(F32)
    flat = jnp.concatenate([total.astype(BF16).reshape(HALF * 32, COUT), jnp.zeros((32, COUT), BF16)], axis=0)
    zy_send[...] = dot_nt(one_hot(COUT, COUT, lambda r, c: r == c), flat).astype(BF16)
    zy_copy = [
        remote(
            zy_send.at[pl.ds(pl.multiple_of(y_at[d] * 16, 16), 16), :],
            zy_recv.at[d - 1], zy_ssem.at[d - 1], zy_rsem.at[d - 1], y_peer[d],
        )
        for d in range(1, SIDE)
    ]
    for copy in zy_copy:
        copy.start()

    halos[2].wait_recv()
    halos[3].wait_recv()
    for b in range(BLOCKS):
        extra = adj_low[b] if b < RIM else adj_up[b - RIM]
        lb = live[b].astype(F32)
        total = target_sum(RIM + b) + extra.astype(F32)
        input_grad[b] = (total * jnp.concatenate([lb, lb], axis=1)).astype(BF16)

    grad_done = pltpu.make_async_copy(input_grad, input_grad_hbm, out_sem.at[1])
    grad_done.start()

    for copy in yz_copy:
        copy.wait_recv()
    total = yz_send[pl.ds(pl.multiple_of(z * 32, 32), 32), :].astype(F32)
    for d in range(1, SIDE):
        total = total + yz_recv[d - 1].astype(F32)
    first = dot(total.astype(BF16), pick_y[...])
    for copy in zy_copy:
        copy.wait_recv()
    total = zy_send[pl.ds(pl.multiple_of(y * 16, 16), 16), :].astype(F32)
    for d in range(1, SIDE):
        total = total + zy_recv[d - 1].astype(F32)
    second = dot(total.astype(BF16), pick_z[...])
    for i in range(SIDE):
        hi, lo = i // 2, i % 2
        x_send[i] = (
            first[hi * 8 : hi * 8 + 8, lo * 128 : lo * 128 + 128]
            + second[lo * 8 : lo * 8 + 8, hi * 128 : hi * 128 + 128]
        )
    x_copy = [
        remote(x_send.at[at], x_recv.at[n], x_ssem.at[n], x_rsem.at[n], to)
        for n, (at, to) in enumerate(x_peer[1:])
    ]
    for copy in x_copy:
        copy.start()
    for copy in x_copy:
        copy.wait_recv()
    mine = x_send[x]
    for d in range(1, SIDE):
        mine = mine + x_recv[2 * d - 1]
    theirs = x_recv[0]
    for d in range(1, SIDE):
        theirs = theirs + x_recv[2 * d]
    pieces[core] = mine
    pieces[1 - core] = theirs

    conv_done.wait()
    grad_done.wait()
    for copy in halos + y_copy + z_copy + yz_copy + zy_copy + x_copy:
        copy.wait_send()

    def sent(j, carry):
        to_mate(j).wait_send()
        return carry

    lax.fori_loop(0, SLOTS, sent, 0)


def target_order(idx):
    number = jnp.arange(PAIRS, dtype=jnp.int32)
    key = idx * 512 + number
    rank = jnp.sum((key[None, :] < key[:, None]).astype(jnp.int32), axis=1)
    order = jnp.sum(jnp.where(rank[:, None] == number[None, :], number[:, None], 0), axis=0)
    target = jnp.arange(ZERO + 1, dtype=jnp.int32)
    ends = jnp.sum((idx[:, None] < target[None, :]).astype(jnp.int32), axis=0)
    return order, ends


def per_device(features, voxel_mask, block_pairs, cotangent, weight):
    links = block_pairs.reshape(PAIRS)
    idx = jnp.where(links == 3 * BLOCKS, ZERO, links - RIM)
    order, ends = target_order(idx)
    idx = jnp.concatenate([idx, jnp.full((BLOCKS,), ZERO, jnp.int32)])

    smem = pl.BlockSpec(memory_space=pltpu.SMEM)
    vmem = pl.BlockSpec(memory_space=pltpu.VMEM)
    hbm = pl.BlockSpec(memory_space=pltpu.HBM)
    dma = pltpu.SemaphoreType.DMA
    conv_out, input_grad, pieces = pl.pallas_call(
        main_kernel,
        out_shape=(
            jax.ShapeDtypeStruct((BLOCKS, VOX, COUT), BF16),
            jax.ShapeDtypeStruct((BLOCKS, VOX, CIN), BF16),
            jax.ShapeDtypeStruct((2, 8, 128), F32),
        ),
        in_specs=[smem] * 3 + [hbm] * 4,
        out_specs=(hbm, hbm, vmem),
        scratch_shapes=[
            pltpu.VMEM((BLOCKS, VOX, COUT), BF16),
            pltpu.VMEM((BLOCKS, VOX, CIN), BF16),
            pltpu.VMEM((1, BLOCKS, VOX, CIN), BF16),
            pltpu.VMEM((BLOCKS, 1, VOX), jnp.int32),
            pltpu.VMEM((1, BLOCKS, VOX, COUT), BF16),
            pltpu.VMEM((OFFSETS, CIN, COUT), BF16),
            pltpu.VMEM((BLOCKS, VOX, COUT), BF16),
            pltpu.VMEM((ZERO + 1, VOX, CIN), BF16),
            pltpu.VMEM((ROWS, COUT), BF16),
            pltpu.VMEM((COUT, ROWS), BF16),
            pltpu.VMEM((PAIRS, VOX, CIN), BF16),
            pltpu.VMEM((PAIRS, VOX, CIN), F32),
            pltpu.VMEM((RIM, VOX, CIN), BF16),
            pltpu.VMEM((RIM, VOX, CIN), BF16),
            pltpu.VMEM((RIM, VOX, CIN), BF16),
            pltpu.VMEM((RIM, VOX, CIN), BF16),
            pltpu.VMEM((ROWS, COUT), F32),
            pltpu.VMEM((CIN, CIN), BF16),
            pltpu.VMEM((128, 256), BF16),
            pltpu.VMEM((256, 512), BF16),
            pltpu.VMEM((SLOTS, COUT, CIN), BF16),
            pltpu.VMEM((SLOTS, COUT, CIN), BF16),
            pltpu.VMEM((HALF, COUT, CIN), BF16),
            pltpu.VMEM((SIDE - 1, HALF, 16, CIN), BF16),
            pltpu.VMEM((HALF, CIN, COUT), BF16),
            pltpu.VMEM((SIDE - 1, HALF, 32, COUT), BF16),
            pltpu.VMEM((CIN, 128), BF16),
            pltpu.VMEM((SIDE - 1, 32, 128), BF16),
            pltpu.VMEM((COUT, 256), BF16),
            pltpu.VMEM((SIDE - 1, 16, 256), BF16),
            pltpu.VMEM((SIDE, 8, 128), F32),
            pltpu.VMEM((15, 8, 128), F32),
            dma((4,)), dma((2,)), dma((4,)), dma((4,)), dma((SLOTS,)), dma((SLOTS,)),
            dma((3, 7)), dma((3, 7)), dma((3, 7)), dma((3, 7)),
            dma((7,)), dma((7,)), dma((7,)), dma((7,)),
            dma((15,)), dma((15,)),
        ],
        compiler_params=pltpu.CompilerParams(
            collective_id=0, has_side_effects=True, vmem_limit_bytes=63 * 1024 * 1024
        ),
        name="conv_and_sums",
    )(idx, order, ends, features, voxel_mask.reshape(BLOCKS, 1, VOX), cotangent, weight)

    core = lax.axis_index("dp") % 2
    by_y = lax.dynamic_index_in_dim(pieces[:, :, :64].reshape(2, 8, 8, 2, 4), core, 3, keepdims=False)
    by_z = lax.dynamic_index_in_dim(pieces[:, :, 64:].reshape(2, 2, 4, 8, 8), core, 1, keepdims=False)
    share = jnp.concatenate(
        [by_y.transpose(0, 2, 1, 3)[:, :HALF], by_z.transpose(0, 2, 3, 1)[:, :HALF]], axis=1
    ).reshape(2 * SLOTS, 8, 4)[:OFFSETS]
    count = lax.axis_size("dp") * lax.axis_size("slab") * ROWS
    weight_grad = share / jnp.float32(math.sqrt(count))
    return (conv_out[None], input_grad[None], weight_grad)


def solution(mesh):
    placed = (
        P("dp", "slab", None, None),
        P("dp", "slab", None),
        P("dp", "slab", None, None),
        P("dp", "slab", None, None),
        P(),
    )
    return jax.shard_map(
        per_device,
        mesh=mesh,
        in_specs=placed,
        out_specs=(P("dp", "slab", None, None), P("dp", "slab", None, None), P(None, "slab", "dp")),
        check_vma=False,
    )
```

time: 84.5 us -> 75.5 us (0.89)
  Pallas kernels: 74.2 us -> 66.1 us
  other arithmetic: 4.38 us -> 2.35 us
  local copies, waits for them, and re-layouts: 4.72 us -> 6.02 us
    pallas_call x2 -> x1, Pallas kernels: 74.2 us -> 66.1 us  [per_device(): pl.pallas_call(main_kernel, out_shape=(jax.ShapeDtypeStruct((BLOCKS, VOX,...]
    mul x2 -> x0, other arithmetic: 2.18 us -> none  [the longest x1 1.12 us: per_device(): masked = features[0] * active]
    reduce_sum x0 -> x3, other arithmetic: none -> 1.56 us  [the longest x1 0.71 us: target_order(): jnp.sum(jnp.where(rank[:, None] == number[None, :], number[:, None], 0),...]
    convert_element_type x2 -> x0, other arithmetic: 1.42 us -> none  [per_device(): active = voxel_mask.reshape(BLOCKS, VOX, 1).astype(BF16)]
    unnamed x8 -> x3, local copies, waits for them, and re-layouts: 3.48 us -> 3.92 us
where the time goes in v2:
time: 75.5 us; the launch traced here: 75.1 us
  Pallas kernels  66.1 us (88%)
  local copies, waits for them, and re-layouts  6.02 us (8%)
  other arithmetic  2.35 us (3%)
    pallas_call x1, Pallas kernels, per_device(): pl.pallas_call(main_kernel, out_shape=(jax.ShapeDtypeStruct((BLOCKS, VOX,...  66.1 us
    unnamed x3, local copies, waits for them, and re-layouts  3.92 us

profile of v2, /device:TPU:1, one launch (start us, length us, event | category | flops | bytes accessed | tf_op | source)
XLA Modules:
  0.0 75.1 jit_solution(12742842051237232538)
XLA Ops:
  0.6 0.7 compare_select_fusion
  1.3 0.1 copy.20
  1.4 0.1 select_n.36
  1.5 0.6 concatenate.6.idx
  2.1 0.2 convert_reduce_fusion
  2.3 0.7 select_reduce_fusion.order
  3.1 0.6 convert_reduce_fusion.1.ends
  3.7 66.1 %conv_and_sums.1 = (bf16[10,64,128]{2,1,0:T(8,128)(2,1)}, bf16[10,64,256]{2,1,0:T(8,128)(2,1)}, f32[2,8,128]{2,1,0:T(8,128)}) custom-call(s32[280]{0:T(512)} %concatenate.6.idx, s32[270]{0:T(512)} %select_reduce_fusion.order, s32[21]{0:T(128)} %convert_reduce_fusion.1.ends, bf16[1,10,64,256]{3,2,1,0:T(8,128)(2,1)} %features_hbm.1, s32[10,1,64]{2,1,0:T(1,128)} %bitcast.21, ...), custom_call_target="tpu_custom_call" | custom-call | tf_op jit(solution)/shard_map/conv_and_sums/pallas_call | solution.py:335
  69.8 0.8 %fusion = (f32[2,8,64]{2,1,0:T(8,128)S(1)}, f32[2,8,64]{2,1,0:T(8,128)S(1)}) fusion(f32[2,8,128]{2,1,0:T(8,128)} %get-tuple-element.8), kind=kLoop, calls=%fused_computation.11 | loop fusion | bytes 16384 | tf_op jit(solution)/shard_map/slice | solution.py:389
  70.6 0.1 reshape.63
  70.7 0.1 copy.24
  70.8 0.1 copy.21
  70.9 0.1 copy.22
  71.0 0.1 pad_maximum_fusion
  71.1 0.1 reshape.64
  71.2 0.6 copy.26
  71.8 1.6 %copy.30 = bf16[1,10,64,128]{3,2,1,0:T(8,128)(2,1)} copy(bf16[1,10,64,128]{3,2,1,0:T(8,128)(2,1)} %bitcast.17) | data formatting | bytes 327680
  73.4 1.7 %copy.31 = bf16[1,10,64,256]{3,2,1,0:T(8,128)(2,1)} copy(bf16[1,10,64,256]{3,2,1,0:T(8,128)(2,1)} %bitcast.16) | data formatting | bytes 655360
  (5 shorter events, 0.1 us)

commit v3 on v2

--- a/solution.py
+++ b/solution.py
@@ -45,7 +45,7 @@
     conv_hbm, input_grad_hbm, pieces,
     conv_out, input_grad, features, mask, cotangent, weight, live, ext, grad, grad_t, term, run, rim_low, rim_up, adj_low, adj_up, conv_acc,
     by_z, pick_y, pick_z, core_send, core_recv, y_send, y_recv, z_send, z_recv,
-    yz_send, yz_recv, zy_send, zy_recv, x_send, x_recv,
+    yz_send, yz_recv, zy_send, zy_recv, x_send, x_recv, x_sum, x_other,
     load_sem, out_sem, halo_ssem, halo_rsem, core_ssem, core_rsem,
     y_ssem, y_rsem, z_ssem, z_rsem, yz_ssem, yz_rsem, zy_ssem, zy_rsem, x_ssem, x_rsem,
 ):
@@ -66,14 +66,14 @@
     x_at = [(x + d) % SIDE for d in range(SIDE)]
     y_peer = [device(y_at[d], x, z, core) for d in range(SIDE)]
     z_peer = [device(y, x, z_at[d], core) for d in range(SIDE)]
-    x_peer = [(x_at[d], device(y, x_at[d], z, (core + c) % 2)) for d in range(SIDE) for c in range(2)]
+    x_peer = [device(y, x_at[d], z, core) for d in range(SIDE)]
 
     pairs = ((mask_hbm, mask), (features_hbm, features), (cotangent_hbm, cotangent), (weight_hbm, weight))
     loads = [pltpu.make_async_copy(src, dst, load_sem.at[n]) for n, (src, dst) in enumerate(pairs)]
     for load in loads:
         load.start()
     barrier = pltpu.get_barrier_semaphore()
-    others = [above, below] + y_peer[1:] + z_peer[1:] + [p for _, p in x_peer[1:]]
+    others = [mate, above, below] + y_peer[1:] + z_peer[1:] + x_peer[1:]
     for other in others:
         pl.semaphore_signal(barrier, inc=1, device_id=other, device_id_type=MESH)
 
@@ -140,6 +140,8 @@
         rim_up[i] = target_sum(RIM + BLOCKS + i).astype(BF16)
     halos[0].wait_recv()
     halos[1].wait_recv()
+    halos[2].start()
+    halos[3].start()
 
     def picked(k, first, last):
         return jnp.concatenate([ext[idx[k * BLOCKS + b]] for b in range(first, last)], axis=0)
@@ -197,8 +199,6 @@
             )
             copy.start()
             z_copy.append(copy)
-    halos[2].start()
-    halos[3].start()
 
     conv_acc[...] = jnp.zeros_like(conv_acc)
 
@@ -284,8 +284,8 @@
             + second[lo * 8 : lo * 8 + 8, hi * 128 : hi * 128 + 128]
         )
     x_copy = [
-        remote(x_send.at[at], x_recv.at[n], x_ssem.at[n], x_rsem.at[n], to)
-        for n, (at, to) in enumerate(x_peer[1:])
+        remote(x_send.at[x_at[d]], x_recv.at[d - 1], x_ssem.at[d - 1], x_rsem.at[d - 1], x_peer[d])
+        for d in range(1, SIDE)
     ]
     for copy in x_copy:
         copy.start()
@@ -293,12 +293,14 @@
         copy.wait_recv()
     mine = x_send[x]
     for d in range(1, SIDE):
-        mine = mine + x_recv[2 * d - 1]
-    theirs = x_recv[0]
-    for d in range(1, SIDE):
-        theirs = theirs + x_recv[2 * d]
+        mine = mine + x_recv[d - 1]
+    x_sum[...] = mine
+    swap = remote(x_sum, x_other, x_ssem.at[7], x_rsem.at[7], mate)
+    swap.start()
+    x_copy.append(swap)
     pieces[core] = mine
-    pieces[1 - core] = theirs
+    swap.wait_recv()
+    pieces[1 - core] = x_other[...]
 
     conv_done.wait()
     grad_done.wait()
@@ -373,14 +375,16 @@
             pltpu.VMEM((COUT, 256), BF16),
             pltpu.VMEM((SIDE - 1, 16, 256), BF16),
             pltpu.VMEM((SIDE, 8, 128), F32),
-            pltpu.VMEM((15, 8, 128), F32),
+            pltpu.VMEM((7, 8, 128), F32),
+            pltpu.VMEM((8, 128), F32),
+            pltpu.VMEM((8, 128), F32),
             dma((4,)), dma((2,)), dma((4,)), dma((4,)), dma((SLOTS,)), dma((SLOTS,)),
             dma((3, 7)), dma((3, 7)), dma((3, 7)), dma((3, 7)),
             dma((7,)), dma((7,)), dma((7,)), dma((7,)),
-            dma((15,)), dma((15,)),
+            dma((8,)), dma((8,)),
         ],
         compiler_params=pltpu.CompilerParams(
-            collective_id=0, has_side_effects=True, vmem_limit_bytes=63 * 1024 * 1024
+            collective_id=0, has_side_effects=True, vmem_limit_bytes=53 * 1024 * 1024
         ),
         name="conv_and_sums",
     )(idx, order, ends, features, voxel_mask.reshape(BLOCKS, 1, VOX), cotangent, weight)

time: 75.5 us -> 71.5 us (0.947)
  local copies, waits for them, and re-layouts: 6.02 us -> 4.35 us
  Pallas kernels: 66.1 us -> 64.9 us
  other arithmetic: 2.35 us -> 1.25 us
    pallas_call x1, Pallas kernels: 66.1 us -> 64.9 us  [per_device(): pl.pallas_call(main_kernel, out_shape=(jax.ShapeDtypeStruct((BLOCKS, VOX,...]
    slice x2, local copies, waits for them, and re-layouts: 0.94 us -> 0.16 us  [per_device(): pieces[:, :, :64].reshape(2, 8, 8, 2, 4)]
    unnamed x3 -> x7, local copies, waits for them, and re-layouts: 3.92 us -> 3.61 us
where the time goes in v3:
time: 71.5 us; the launch traced here: 71.2 us
  Pallas kernels  64.9 us (91%)
  local copies, waits for them, and re-layouts  4.35 us (6%)
  other arithmetic  1.25 us (2%)
  between operations  0.73 us (1%)
    pallas_call x1, Pallas kernels, per_device(): pl.pallas_call(main_kernel, out_shape=(jax.ShapeDtypeStruct((BLOCKS, VOX,...  64.9 us
    unnamed x7, local copies, waits for them, and re-layouts  3.61 us

profile of v3, /device:TPU:1, one launch (start us, length us, event | category | flops | bytes accessed | tf_op | source)
XLA Modules:
  0.0 71.2 jit_solution(4500792389515510409)
XLA Ops:
  0.6 0.7 compare_select_fusion
  1.3 0.1 copy.20
  1.4 0.1 select_n.36
  1.6 0.2 convert_reduce_fusion
  1.8 0.1 select_reduce_fusion.order
  1.9 0.1 convert_reduce_fusion.1.ends
  2.0 0.0 copy-start
  2.0 0.9 %copy-done = bf16[1,10,64,128]{3,2,1,0:T(8,128)(2,1)S(1)} copy-done((bf16[1,10,64,128]{3,2,1,0:T(8,128)(2,1)S(1)}, bf16[1,10,64,128]{3,2,1,0:T(8,128)(2,1)}, u32[]{:S(2)}) %copy-start) | copy-done | bytes 163864
  2.9 0.0 copy-start.1
  2.9 0.7 copy-done.1
  3.6 64.9 %conv_and_sums.1 = (bf16[10,64,128]{2,1,0:T(8,128)(2,1)S(1)}, bf16[10,64,256]{2,1,0:T(8,128)(2,1)S(1)}, f32[2,8,128]{2,1,0:T(8,128)S(1)}) custom-call(s32[280]{0:T(512)S(1)} %concatenate.6.idx, s32[270]{0:T(512)S(1)} %select_reduce_fusion.order, s32[21]{0:T(128)S(1)} %convert_reduce_fusion.1.ends, bf16[1,10,64,256]{3,2,1,0:T(8,128)(2,1)} %features_hbm.1, ...), custom_call_target="tpu_custom_call" | custom-call | tf_op jit(solution)/shard_map/conv_and_sums/pallas_call | solution.py:337
  68.5 0.1 fusion
  68.6 0.1 reshape.63
  68.7 0.1 copy.24
  68.8 0.1 copy.21
  68.9 0.1 copy.22
  69.0 0.1 pad_maximum_fusion
  69.1 0.1 reshape.64
  69.2 0.6 copy.26
  69.8 0.7 copy.30
  70.5 0.7 %copy.31 = bf16[1,10,64,256]{3,2,1,0:T(8,128)(2,1)} copy(bf16[1,10,64,256]{3,2,1,0:T(8,128)(2,1)S(1)} %bitcast.16) | data formatting | bytes 655360
  (6 shorter events, 0.1 us)
Async XLA Ops:
  2.0 0.9 %copy-start = (bf16[1,10,64,128]{3,2,1,0:T(8,128)(2,1)S(1)}, bf16[1,10,64,128]{3,2,1,0:T(8,128)(2,1)}, u32[]{:S(2)}) copy-start(bf16[1,10,64,128]{3,2,1,0:T(8,128)(2,1)} %cotangent_hbm.1) | copy-start | bytes 491524
  2.9 0.7 copy-start.1
